TPU v7x, 32 devices: a whole 2x2x4 slice. The times are simulated.
32 devices in a mesh: group: 4 (over z), req: 8 (over y, x, core).
Axes of the slice: x: 2, y: 2, z: 4, core: 2. Of those that a mesh axis runs over, the one named last changes fastest.
Arguments:
- layer_input: bfloat16 [4096, 3072], P(('group', 'req')), may hold values from -6 to 6
- queries: bfloat16 [4096, 3072], P(('group', 'req')), may hold values from -240 to 240, as said below
- suffix_kv: bfloat16 [4096, 2048], P(('group', 'req')), may hold values from -6 to 6
- past_kv: bfloat16 [8192, 2048], P(('group', 'req')), may hold values from -6 to 6
- prefix_kv: bfloat16 [512, 2048], P(('group', 'req')), may hold values from -6 to 6
- suffix_len: int32 [32], P(('group', 'req')), may hold values from 1 to 128, 3072 in all
- past_len: int32 [32], P(('group', 'req')), may hold values from 1 to 256, 4096 in all
- out_weight: bfloat16 [3072, 3072], P('group'), may hold values from -0.109375 to 0.109375
- norm_gain: bfloat16 [3072], replicated, may hold values from 0.5 to 1.5
- gate_weight: bfloat16 [3072, 8192], P(None, 'req'), may hold values from -0.109375 to 0.109375
- up_weight: bfloat16 [3072, 8192], P(None, 'req'), may hold values from -0.109375 to 0.109375
- down_weight: bfloat16 [8192, 3072], P('req'), may hold values from -0.0625 to 0.0625
Outputs:
- layer_output: bfloat16 [4096, 3072], P(('group', 'req'))
Inputs may be any that keep to these rules, and one draw needn't show every extreme that they name: `queries`: normally distributed entries; some rows may be far larger.
All inputs are finite; a program needn't handle non-finite values. No bound on the sum of `suffix_len` or of `past_len` on one device may be relied on, other than what follows from the above.
Results may differ from a plain program's by a relative error of at most 0.012.
Values may be sent and summed in bfloat16 or wider, within the bound.
A program may use at most 128 MiB of HBM per device.

v0:
```python
import jax
import jax.numpy as jnp
from jax import lax
from jax.sharding import PartitionSpec as P

HEADS = 24
KV_HEADS = 8
HEAD = 128
SINK = 4


def absorb(state, query_heads, key_rows, key_pos, key_valid, query_pos, window):
    maxima, totals, sums = state
    count = key_rows.shape[0]
    key_heads = key_rows[:, : KV_HEADS * HEAD].reshape(count, KV_HEADS, HEAD)
    value_heads = key_rows[:, KV_HEADS * HEAD :].reshape(count, KV_HEADS, HEAD)
    scores = jnp.einsum(
        "skgh,nkh->kgsn", query_heads, key_heads, preferred_element_type=jnp.float32
    ) * HEAD ** (-0.5)
    near = query_pos[:, None] - key_pos[None, :] < window
    allowed = (
        key_valid[None, :]
        & (key_pos[None, :] <= query_pos[:, None])
        & ((key_pos[None, :] < SINK) | near)
    )
    scores = jnp.where(allowed, scores, -1e30)
    new_max = jnp.maximum(maxima, jnp.max(scores, axis=-1))
    expo = jnp.where(allowed, jnp.exp(scores - new_max[..., None]), 0.0)
    factor = jnp.exp(maxima - new_max)
    totals = totals * factor + jnp.sum(expo, axis=-1)
    sums = sums * factor[..., None] + jnp.einsum(
        "kgsn,nkh->kgsh", expo.astype(jnp.bfloat16), value_heads, preferred_element_type=jnp.float32
    )
    return (new_max, totals, sums)


def shards(
    layer_input,
    queries,
    suffix_kv,
    past_kv,
    prefix_kv,
    suffix_len,
    past_len,
    out_weight,
    norm_gain,
    gate_weight,
    up_weight,
    down_weight,
):
    rows_here = queries.shape[0]
    past_slots = past_kv.shape[0]
    prefix_total = prefix_kv.shape[0] * lax.axis_size("req")
    window = prefix_total + past_slots // 2
    past_count = past_len[0]
    offsets = jnp.arange(rows_here, dtype=jnp.int32)
    query_pos = prefix_total + past_count + offsets
    ratio = HEADS // KV_HEADS
    query_heads = queries.reshape(rows_here, KV_HEADS, ratio, HEAD)
    state = (
        jnp.full((KV_HEADS, ratio, rows_here), -1e30, jnp.float32),
        jnp.zeros((KV_HEADS, ratio, rows_here), jnp.float32),
        jnp.zeros((KV_HEADS, ratio, rows_here, HEAD), jnp.float32),
    )
    local_rows = jnp.concatenate([past_kv, suffix_kv], axis=0)
    local_pos = jnp.concatenate([prefix_total + jnp.arange(past_slots, dtype=jnp.int32), query_pos])
    local_valid = jnp.concatenate(
        [jnp.arange(past_slots, dtype=jnp.int32) < past_count, jnp.ones((rows_here,), bool)]
    )
    state = absorb(state, query_heads, local_rows, local_pos, local_valid, query_pos, window)
    piece = lax.all_gather(prefix_kv, "req", axis=0, tiled=True)
    count = piece.shape[0]
    positions = jnp.arange(count, dtype=jnp.int32)
    maxima, totals, sums = absorb(
        state, query_heads, piece, positions, jnp.ones((count,), bool), query_pos, window
    )
    attended = (
        (sums / totals[..., None])
        .transpose(2, 0, 1, 3)
        .reshape(rows_here, HEADS * HEAD)
        .astype(jnp.bfloat16)
    )
    blocks = lax.axis_size("group")
    split_rows = attended.reshape(rows_here, blocks, attended.shape[1] // blocks)
    received = lax.all_to_all(split_rows, "group", split_axis=1, concat_axis=0, tiled=True)
    received = received.reshape(blocks * rows_here, attended.shape[1] // blocks)
    picked = received
    projected = lax.psum_scatter(
        jnp.dot(picked, out_weight, preferred_element_type=jnp.float32).astype(jnp.bfloat16),
        "group",
        scatter_dimension=0,
        tiled=True,
    ).astype(jnp.float32)
    mixed = layer_input.astype(jnp.float32) + projected
    scale = lax.rsqrt(jnp.mean(mixed * mixed, axis=-1, keepdims=True) + 1e-05)
    normed = (mixed * scale * norm_gain.astype(jnp.float32)).astype(jnp.bfloat16)
    gathered = lax.all_gather(normed, "req", axis=0, tiled=True)
    picked = gathered
    gate = jnp.dot(picked, gate_weight, preferred_element_type=jnp.float32)
    upper = jnp.dot(picked, up_weight, preferred_element_type=jnp.float32)
    hidden = (jax.nn.silu(gate) * upper).astype(jnp.bfloat16)
    feed = lax.psum_scatter(
        jnp.dot(hidden, down_weight, preferred_element_type=jnp.float32).astype(jnp.bfloat16),
        "req",
        scatter_dimension=0,
        tiled=True,
    ).astype(jnp.float32)
    live = offsets < suffix_len[0]
    return jnp.where(live[:, None], mixed + feed, 0.0).astype(jnp.bfloat16)


def solution(mesh):
    in_specs = (
        P(("group", "req"), None),
        P(("group", "req"), None),
        P(("group", "req"), None),
        P(("group", "req"), None),
        P(("group", "req"), None),
        P(("group", "req")),
        P(("group", "req")),
        P("group", None),
        P(),
        P(None, "req"),
        P(None, "req"),
        P("req", None),
    )
    out_specs = P(("group", "req"), None)
    return jax.shard_map(shards, mesh=mesh, in_specs=in_specs, out_specs=out_specs, check_vma=False)
```

profile of v0, /device:TPU:0, one launch (start us, length us, event | category | flops | bytes accessed | tf_op | source)
XLA Modules:
  0.0 270.3 jit_solution(1269483766876913524)
XLA Ops:
  7.3 1.5 copy.30
  8.8 1.3 copy.31
  10.2 0.4 copy.32
  10.6 11.3 %all_gather.6 = bf16[128,2048]{1,0:T(8,128)(2,1)S(1)} all-gather(bf16[16,2048]{1,0:T(8,128)(2,1)S(1)} %copy-done.3), channel_id=1, replica_groups=mesh['group'=4,'req'=8] {'req'}, dimensions={0}, use_global_device_ids=true | all-gather | bytes 589824 | tf_op jit(solution)/shard_map/all_gather | solution.py:71
  22.6 0.9 fusion
  23.5 0.4 fusion.35
  23.9 1.2 fusion.1
  25.1 2.5 fusion.3
  27.8 0.3 fusion.13
  28.1 1.9 fusion.11
  30.1 0.3 copy.41
  30.3 25.3 %all_to_all.15 = bf16[128,4,768]{2,0,1:T(8,128)(2,1)S(1)} all-to-all(bf16[128,4,768]{2,0,1:T(8,128)(2,1)S(1)} %copy.41), channel_id=1, replica_groups=mesh['group'=4,'req'=8] {'group'}, dimensions={1} | all-to-all | bytes 1572864 | tf_op jit(solution)/shard_map/all_to_all | solution.py:85
  55.6 6.3 %convolution_convert_fusion.1 = bf16[512,3072]{1,0:T(8,128)(2,1)} fusion(bf16[512,768]{1,0:T(8,128)(2,1)S(1)} %bitcast.97, bf16[768,3072]{1,0:T(8,128)(2,1)} %param.19), kind=kOutput, calls=%fused_computation.3 | convolution fusion | flops 2417491968 | bytes 8650752 | tf_op jit(solution)/shard_map/dot_general | solution.py:89
  62.0 0.6 copy-done.4
  62.6 57.9 %reduce-scatter.3.cloned.1.call-done = bf16[128,3072]{1,0:T(8,128)(2,1)} async-done(((bf16[512,3072]{1,0:T(8,128)(2,1)}), bf16[128,3072]{1,0:T(8,128)(2,1)}) %reduce-scatter.3.cloned.1.call-update) | async-done | bytes 786448 | tf_op jit(solution)/shard_map/reduce_scatter | solution.py:88
  120.5 1.5 multiply_reduce_fusion
  122.0 2.3 multiply_convert_fusion.1
  124.3 0.2 reduce-scatter.5.cloned.1.call-start
  124.6 45.5 %all-gather.2.cloned.1.call-done = bf16[1024,3072]{1,0:T(8,128)(2,1)} async-done(((bf16[128,3072]{1,0:T(8,128)(2,1)}), bf16[1024,3072]{1,0:T(8,128)(2,1)}) %all-gather.2.cloned.1.call-update) | async-done | bytes 6291472 | tf_op jit(solution)/shard_map/all_gather | solution.py:97
  170.1 11.3 %fusion.36 = f32[1024,1024]{1,0:T(8,128)S(1)} fusion(bf16[1024,3072]{1,0:T(8,128)(2,1)} %all-gather.2.cloned.1.call-done, bf16[3072,1024]{1,0:T(8,128)(2,1)} %param.21), kind=kOutput, calls=%fused_computation.65 | convolution fusion | flops 6442450944 | bytes 16777216 | tf_op jit(solution)/shard_map/dot_general | solution.py:99
  181.4 9.4 %multiply_convert_fusion = bf16[1024,1024]{1,0:T(8,128)(2,1)S(1)} fusion(f32[1024,1024]{1,0:T(8,128)S(1)} %fusion.36, bf16[1024,3072]{1,0:T(8,128)(2,1)S(1)} %copy-done.5, bf16[3072,1024]{1,0:T(8,128)(2,1)} %param.22), kind=kOutput, calls=%fused_computation.4 | convolution fusion | flops 6448742400 | bytes 18874368 | tf_op jit(solution)/shard_map/dot_general | solution.py:100
  190.8 8.7 %convolution_convert_fusion = bf16[1024,3072]{1,0:T(8,128)(2,1)} fusion(bf16[1024,1024]{1,0:T(8,128)(2,1)S(1)} %multiply_convert_fusion, bf16[1024,3072]{1,0:T(8,128)(2,1)S(1)} %bitcast.101), kind=kOutput, calls=%fused_computation | convolution fusion | flops 6445596672 | bytes 14680064 | tf_op jit(solution)/shard_map/dot_general | solution.py:103
  200.2 61.2 %reduce-scatter.5.cloned.1.call-done = bf16[128,3072]{1,0:T(8,128)(2,1)} async-done(((bf16[1024,3072]{1,0:T(8,128)(2,1)}), bf16[128,3072]{1,0:T(8,128)(2,1)}) %reduce-scatter.5.cloned.1.call-update) | async-done | bytes 786448 | tf_op jit(solution)/shard_map/reduce_scatter | solution.py:102
  261.4 2.4 select_convert_fusion
  (39 shorter events, 1.1 us)
Async XLA Ops:
  6.5 3.6 %copy-start.2 = (bf16[128,3072]{1,0:T(8,128)(2,1)S(1)}, bf16[128,3072]{1,0:T(8,128)(2,1)}, u32[]{:S(2)}) copy-start(bf16[128,3072]{1,0:T(8,128)(2,1)} %param.13) | copy-start | bytes 2359300
  6.5 4.1 %copy-start.3 = (bf16[16,2048]{1,0:T(8,128)(2,1)S(1)}, bf16[16,2048]{1,0:T(8,128)(2,1)}, u32[]{:S(2)}) copy-start(bf16[16,2048]{1,0:T(8,128)(2,1)} %param.16) | copy-start | bytes 196612
  6.5 114.0 %reduce-scatter.3.cloned.1.call-start = ((), (), s32[]{:S(2)}) async-start(), calls=%async_computation.3 | async-start | bytes 3932160 | tf_op jit(solution)/shard_map/reduce_scatter | solution.py:88
  61.9 0.7 copy-start.4
  61.9 58.6 %copy-start = (bf16[128,3072]{1,0:T(8,128)(2,1)S(1)}, bf16[128,3072]{1,0:T(8,128)(2,1)}, u32[]{:S(2)}) copy-start(bf16[128,3072]{1,0:T(8,128)(2,1)} %param.12) | copy-start | bytes 2359300
  61.9 108.1 %all-gather.2.cloned.1.call-start = ((), (), s32[]{:S(2)}) async-start(), calls=%async_computation.4 | async-start | bytes 7077888 | tf_op jit(solution)/shard_map/all_gather | solution.py:97
  124.3 137.1 %reduce-scatter.5.cloned.1.call-start = ((), (), s32[]{:S(2)}) async-start(), calls=%async_computation.5 | async-start | bytes 7077888 | tf_op jit(solution)/shard_map/reduce_scatter | solution.py:102
  170.1 11.3 %copy-start.5 = (bf16[1024,3072]{1,0:T(8,128)(2,1)S(1)}, bf16[1024,3072]{1,0:T(8,128)(2,1)}, u32[]{:S(2)}) copy-start(bf16[1024,3072]{1,0:T(8,128)(2,1)} %all-gather.2.cloned.1.call-done) | copy-start | bytes 18874372
  170.1 20.7 %slice-start = ((s8[6291456]{0:T(1024)(128)(4,1)}), s8[4194304]{0:T(1024)(128)(4,1)S(1)}, s32[]{:S(2)}) async-start(s8[6291456]{0:T(1024)(128)(4,1)} %bitcast.100), calls=%async_computation.6 | async-start | bytes 8388608
  181.4 9.4 %slice-start.1 = ((s8[6291456]{0:T(1024)(128)(4,1)}), s8[2097152]{0:T(1024)(128)(4,1)S(1)}, s32[]{:S(2)}) async-start(s8[6291456]{0:T(1024)(128)(4,1)} %bitcast.100), calls=%async_computation.7 | async-start | bytes 4194304
  199.5 61.9 %copy-start.1 = (bf16[128,3072]{1,0:T(8,128)(2,1)S(1)}, bf16[128,3072]{1,0:T(8,128)(2,1)}, u32[]{:S(2)}) copy-start(bf16[128,3072]{1,0:T(8,128)(2,1)} %reduce-scatter.3.cloned.1.call-done) | copy-start | bytes 2359300
Sparse Core Ops, SparseCore 0:
  62.1 58.3 reduce-scatter.2
  124.5 45.5 all-gather.1
  199.6 61.7 reduce-scatter.4
where the time goes:
time: 271 us; the launch traced here: 270 us
  waiting for transfers between devices  165 us (61%)
  matrix products  41.4 us (15%)
  blocking collectives  36.6 us (14%)
  between operations  14.8 us (5%)
  other arithmetic  8.23 us (3%)
  local copies, waits for them, and re-layouts  4.46 us (2%)
    reduce_scatter x1, waiting for transfers between devices, shards(): lax.psum_scatter(jnp.dot(hidden, down_weight, preferred_element_type=jnp....  61.2 us
    reduce_scatter x1, waiting for transfers between devices, shards(): lax.psum_scatter(jnp.dot(picked, out_weight, preferred_element_type=jnp.f...  57.9 us
    all_gather x1, waiting for transfers between devices, shards(): gathered = lax.all_gather(normed, 'req', axis=0, tiled=True)  45.5 us
    all_to_all x1, blocking collectives, shards(): lax.all_to_all(split_rows, 'group', split_axis=1, concat_axis=0, tiled=True)  25.3 us
    all_gather x1, blocking collectives, shards(): piece = lax.all_gather(prefix_kv, 'req', axis=0, tiled=True)  11.3 us
    dot_general x1, matrix products, shards(): gate = jnp.dot(picked, gate_weight, preferred_element_type=jnp.float32)  11.3 us
    dot_general x1, matrix products, shards(): upper = jnp.dot(picked, up_weight, preferred_element_type=jnp.float32)  9.39 us
    dot_general x1, matrix products, shards(): jnp.dot(hidden, down_weight, preferred_element_type=jnp.float32)  8.67 us
  transfers between devices with their start and end apart: 3, of which 3 were waited for; matrix products, arithmetic and copies ran while one was open for 0% of the time, Pallas kernels for 0%

commit v1 on v0

--- a/solution.py
+++ b/solution.py
@@ -1,12 +1,18 @@
+import functools
+
 import jax
 import jax.numpy as jnp
 from jax import lax
+from jax.experimental import pallas as pl
+from jax.experimental.pallas import tpu as pltpu
 from jax.sharding import PartitionSpec as P
 
 HEADS = 24
 KV_HEADS = 8
 HEAD = 128
 SINK = 4
+MESH = pl.DeviceIdType.MESH
+CHUNKS = 2
 
 
 def absorb(state, query_heads, key_rows, key_pos, key_valid, query_pos, window):
@@ -109,6 +115,536 @@
     return jnp.where(live[:, None], mixed + feed, 0.0).astype(jnp.bfloat16)
 
 
+def layer_kernel(
+    n_group,
+    input_hbm,
+    query_hbm,
+    suffix_hbm,
+    past_hbm,
+    prefix_hbm,
+    suffix_len,
+    past_len,
+    outw_hbm,
+    gain_ref,
+    gate_hbm,
+    up_hbm,
+    down_hbm,
+    out_ref,
+    query,
+    rows_kv,
+    bias,
+    residual,
+    out_w,
+    attended,
+    normed,
+    gate_w,
+    up_w,
+    down_w,
+    hidden,
+    row_scale,
+    parts,
+    sums,
+    first,
+    second,
+    local_sem,
+    send_sem,
+    recv_sem,
+    z_send,
+    z_recv,
+):
+    n_req = 8
+    z = lax.axis_index("group")
+    r = lax.axis_index("req")
+    core, x, y = r % 2, (r // 2) % 2, r // 4
+
+    def flip(mask):
+        c2 = 1 - core if mask & 1 else core
+        x2 = 1 - x if mask & 2 else x
+        y2 = 1 - y if mask & 4 else y
+        return y2 * 4 + x2 * 2 + c2
+
+    tokens, width = query.shape
+    rows = tokens // CHUNKS
+    past_slots = past_hbm.shape[0]
+    own_prefix = prefix_hbm.shape[0]
+    prefix = own_prefix * n_req
+    window = prefix + past_slots // 2
+    depth = outw_hbm.shape[0]
+    cols = width // n_req
+    half = width // 2
+    kv_cols = KV_HEADS * HEAD
+    keys = prefix + past_slots + tokens
+
+    def col_slice(owner):
+        return pl.ds(pl.multiple_of(owner * cols, 128), cols)
+
+    def row_slice(owner, count):
+        return pl.ds(pl.multiple_of(owner * count, 16), count)
+
+    used = [0]
+    started = []
+
+    def reserve(count):
+        base = used[0]
+        used[0] += count
+        return base
+
+    def remote(src, dst, index, device):
+        return pltpu.make_async_remote_copy(
+            src_ref=src,
+            dst_ref=dst,
+            send_sem=send_sem.at[index],
+            recv_sem=recv_sem.at[index],
+            device_id={"req": device},
+            device_id_type=MESH,
+        )
+
+    def begin(copy):
+        copy.start()
+        started.append(copy)
+
+    def local(src, dst, index):
+        copy = pltpu.make_async_copy(src, dst, local_sem.at[index])
+        copy.start()
+        return copy
+
+    small = [
+        local(query_hbm, query, 0),
+        local(past_hbm, rows_kv.at[pl.ds(prefix, past_slots)], 1),
+        local(suffix_hbm, rows_kv.at[pl.ds(prefix + past_slots, tokens)], 2),
+        local(prefix_hbm, rows_kv.at[row_slice(r, own_prefix)], 3),
+    ]
+    own_w = local(outw_hbm.at[:, col_slice(r)], out_w.at[row_slice(z, depth)], 4)
+    own_x = local(input_hbm.at[:, col_slice(r)], residual.at[r], 5)
+
+    barrier = pltpu.get_barrier_semaphore()
+    for mask in range(1, n_req):
+        pl.semaphore_signal(barrier, inc=1, device_id={"req": flip(mask)}, device_id_type=MESH)
+    has_left, has_right = z > 0, z < n_group - 1
+
+    @pl.when(has_left)
+    def _():
+        pl.semaphore_signal(barrier, inc=1, device_id={"group": z - 1}, device_id_type=MESH)
+
+    @pl.when(has_right)
+    def _():
+        pl.semaphore_signal(barrier, inc=1, device_id={"group": z + 1}, device_id_type=MESH)
+
+    peers = n_req - 1 + jnp.where(has_left, 1, 0) + jnp.where(has_right, 1, 0)
+    pl.semaphore_wait(barrier, peers)
+
+    prefix_copies = []
+    base = reserve(n_req - 1)
+    for mask in range(1, n_req):
+        copy = remote(prefix_hbm, rows_kv.at[row_slice(r, own_prefix)], base + mask - 1, flip(mask))
+        begin(copy)
+        prefix_copies.append(copy)
+
+    def z_copy(direction, step):
+        block = z - (step - 1) if direction == 0 else z + (step - 1)
+        where = out_w.at[row_slice(block, depth)]
+        src = outw_hbm.at[:, col_slice(r)] if step == 1 else where
+        return pltpu.make_async_remote_copy(
+            src_ref=src,
+            dst_ref=where,
+            send_sem=z_send.at[direction, step - 1],
+            recv_sem=z_recv.at[direction, step - 1],
+            device_id={"group": z + 1 if direction == 0 else z - 1},
+            device_id_type=MESH,
+        )
+
+    def z_sends(direction, step):
+        if direction == 0:
+            return (z - (step - 1) >= 0) & has_right
+        return (z + (step - 1) <= n_group - 1) & has_left
+
+    def z_gets(direction, step):
+        return z - step >= 0 if direction == 0 else z + step <= n_group - 1
+
+    def z_arrived(direction, step):
+        block = z - step if direction == 0 else z + step
+        where = out_w.at[row_slice(block, depth)]
+        pltpu.make_async_remote_copy(
+            src_ref=where,
+            dst_ref=where,
+            send_sem=z_send.at[direction, step - 1],
+            recv_sem=z_recv.at[direction, step - 1],
+            device_id={"req": flip(1)},
+            device_id_type=MESH,
+        ).wait_recv()
+
+    def z_step(step):
+        for direction in (0, 1):
+            if step > 1:
+
+                @pl.when(z_gets(direction, step - 1))
+                def _():
+                    z_arrived(direction, step - 1)
+
+            if step < n_group:
+
+                @pl.when(z_sends(direction, step))
+                def _():
+                    z_copy(direction, step).start()
+
+    z_step(1)
+
+    input_copies = []
+    base = reserve(n_req - 1)
+    for mask in range(1, n_req):
+        other = flip(mask)
+        copy = remote(input_hbm.at[:, col_slice(other)], residual.at[r], base + mask - 1, other)
+        begin(copy)
+        input_copies.append(copy)
+
+    weights = [
+        local(gate_hbm, gate_w, 6),
+        local(up_hbm, up_w, 7),
+        local(down_hbm, down_w, 8),
+    ]
+
+    ratio = HEADS // KV_HEADS
+    past_count = past_len[0]
+    for chunk in range(CHUNKS):
+        key = lax.broadcasted_iota(jnp.int32, (rows, keys), 1)
+        token = lax.broadcasted_iota(jnp.int32, (rows, keys), 0) + chunk * rows
+        query_pos = prefix + past_count + token
+        key_pos = jnp.where(key < prefix + past_slots, key, key - past_slots + past_count)
+        valid = (key < prefix + past_count) | (key >= prefix + past_slots)
+        allowed = valid & (key_pos <= query_pos) & ((key_pos < SINK) | (query_pos - key_pos < window))
+        term = jnp.where(allowed, 0.0, -1e30)
+        for head in range(ratio):
+            bias[chunk, pl.ds(head * rows, rows), :] = term
+
+    for copy in small:
+        copy.wait()
+    for copy in prefix_copies:
+        copy.wait_recv()
+
+    def attend(chunk, group):
+        lanes = pl.multiple_of(group * (ratio * HEAD), 128)
+        mine = jnp.concatenate(
+            [
+                query[pl.ds(chunk * rows, rows), pl.ds(lanes + head * HEAD, HEAD)]
+                for head in range(ratio)
+            ],
+            axis=0,
+        )
+        keys_here = rows_kv[:, pl.ds(pl.multiple_of(group * HEAD, 128), HEAD)]
+        values = rows_kv[:, pl.ds(pl.multiple_of(kv_cols + group * HEAD, 128), HEAD)]
+        scores = lax.dot_general(
+            mine, keys_here, (((1,), (1,)), ((), ())), preferred_element_type=jnp.float32
+        )
+        scores = scores * HEAD ** (-0.5) + bias[chunk]
+        expo = jnp.exp(scores - jnp.max(scores, axis=-1, keepdims=True))
+        denom = jnp.sum(expo, axis=-1, keepdims=True)
+        result = jnp.dot(expo.astype(jnp.bfloat16), values, preferred_element_type=jnp.float32) / denom
+        result = result.astype(jnp.bfloat16)
+        for head in range(ratio):
+            attended[chunk, row_slice(r, rows), pl.ds(lanes + head * HEAD, HEAD)] = result[
+                head * rows : (head + 1) * rows
+            ]
+
+    class Gather:
+        def __init__(self, region):
+            self.region = region
+            base = reserve(14)
+            X, Y, S = flip(2), flip(4), flip(1)
+            plan = [
+                (r, 0, X), (r, 1, Y), (r, 1, X), (r, 0, Y),
+                (X, 0, Y), (Y, 1, X),
+                (r, 0, S), (r, 1, S),
+                (X, 0, S), (Y, 1, S), (X, 1, S), (Y, 0, S),
+                (flip(6), 0, S), (flip(6), 1, S),
+            ]
+            self.copies = [
+                remote(region(owner, rail), region(owner, rail), base + i, device)
+                for i, (owner, rail, device) in enumerate(plan)
+            ]
+
+        def go(self, *which):
+            for i in which:
+                begin(self.copies[i])
+
+        def got(self, *which):
+            for i in which:
+                self.copies[i].wait_recv()
+
+        def forward(self):
+            self.got(0)
+            self.go(4, 8)
+            self.got(1)
+            self.go(5, 9)
+            self.got(2)
+            self.go(10)
+            self.got(3)
+            self.go(11)
+
+        def relay(self):
+            self.got(4)
+            self.go(12)
+            self.got(5)
+            self.go(13)
+
+        def finish(self):
+            self.got(6, 7, 8, 9, 10, 11, 12, 13)
+
+    def attended_region(chunk):
+        return lambda owner, rail: attended.at[chunk, row_slice(owner, rows), pl.ds(rail * half, half)]
+
+    def normed_region(chunk):
+        band = n_req * rows // 2
+        return lambda owner, rail: normed.at[chunk, pl.ds(rail * band, band), col_slice(owner)]
+
+    heads_gather = [Gather(attended_region(chunk)) for chunk in range(CHUNKS)]
+    token_gather = [Gather(normed_region(chunk)) for chunk in range(CHUNKS)]
+
+    for chunk in range(CHUNKS):
+
+        @pl.loop(0, KV_HEADS // 2)
+        def _(group):
+            attend(chunk, group)
+
+        heads_gather[chunk].go(0, 3, 6)
+
+        @pl.loop(KV_HEADS // 2, KV_HEADS)
+        def _(group):
+            attend(chunk, group)
+
+        heads_gather[chunk].go(1, 2, 7)
+
+    z_step(2)
+    heads_gather[0].forward()
+    heads_gather[0].relay()
+    z_step(3)
+    heads_gather[1].forward()
+    heads_gather[1].relay()
+    for copy in input_copies:
+        copy.wait_recv()
+    own_x.wait()
+    own_w.wait()
+    heads_gather[0].finish()
+    heads_gather[1].finish()
+    z_step(4)
+
+    gain_here = gain_ref[:, col_slice(r)].astype(jnp.float32)
+
+    def project(chunk):
+        total = jnp.dot(attended[chunk], out_w[...], preferred_element_type=jnp.float32)
+        total = total + residual[:, pl.ds(chunk * rows, rows), :].astype(jnp.float32).reshape(
+            n_req * rows, cols
+        )
+        normed[chunk, :, col_slice(r)] = (total * gain_here).astype(jnp.bfloat16)
+        token_gather[chunk].go(0, 1, 2, 3, 6, 7)
+
+    def norms(chunk):
+        inverse = 1.0 / gain_ref[...].astype(jnp.float32)
+
+        @pl.loop(0, n_req)
+        def _(block):
+            where = row_slice(block, rows)
+            values = normed[chunk, where, :].astype(jnp.float32) * inverse
+            mean = jnp.sum(values * values, axis=-1, keepdims=True) / width
+            row_scale[where, :] = lax.rsqrt(mean + 1e-05)
+
+    tile = 256
+
+    def widen(chunk, start, stop):
+        @pl.loop(start, stop)
+        def _(i):
+            lanes = pl.ds(pl.multiple_of(i * tile, 128), tile)
+            gate = jnp.dot(normed[chunk], gate_w[:, lanes], preferred_element_type=jnp.float32)
+            upper = jnp.dot(normed[chunk], up_w[:, lanes], preferred_element_type=jnp.float32)
+            scale = row_scale[...]
+            gate = gate * scale
+            hidden[:, lanes] = (gate / (1.0 + jnp.exp(-gate)) * (upper * scale)).astype(jnp.bfloat16)
+
+    def narrow(chunk, rail):
+        step = 512
+
+        @pl.loop(0, half // step)
+        def _(i):
+            lanes = pl.ds(pl.multiple_of(rail * half + i * step, 128), step)
+            part = jnp.dot(hidden[...], down_w[:, lanes], preferred_element_type=jnp.float32)
+            parts[chunk, :, :, :, :, lanes] = part.astype(jnp.bfloat16).reshape(2, 2, 2, rows, step)
+
+    def rail_cols(rail):
+        return pl.ds(rail * half, half)
+
+    def scatter_copies(chunk, rail):
+        lanes = rail_cols(rail)
+        base = reserve(3)
+        to_core = remote(
+            parts.at[chunk, :, :, 1 - core, :, lanes], sums.at[chunk, :, :, :, lanes], base, flip(1)
+        )
+        if rail == 0:
+            far = remote(sums.at[chunk, 1 - y, :, :, lanes], first.at[chunk, rail], base + 1, flip(4))
+            near = remote(sums.at[chunk, y, 1 - x, :, lanes], second.at[chunk, rail], base + 2, flip(2))
+        else:
+            far = remote(sums.at[chunk, :, 1 - x, :, lanes], first.at[chunk, rail], base + 1, flip(2))
+            near = remote(sums.at[chunk, 1 - y, x, :, lanes], second.at[chunk, rail], base + 2, flip(4))
+        return to_core, far, near
+
+    scatter = [[scatter_copies(chunk, rail) for rail in (0, 1)] for chunk in range(CHUNKS)]
+
+    def f32(value):
+        return value.astype(jnp.float32)
+
+    def scatter_core(chunk, rail):
+        begin(scatter[chunk][rail][0])
+
+    def scatter_far(chunk, rail):
+        lanes = rail_cols(rail)
+        scatter[chunk][rail][0].wait_recv()
+        for a in (0, 1):
+            for b in (0, 1):
+                sums[chunk, a, b, :, lanes] = (
+                    f32(sums[chunk, a, b, :, lanes]) + f32(parts[chunk, a, b, core, :, lanes])
+                ).astype(jnp.bfloat16)
+        begin(scatter[chunk][rail][1])
+
+    def scatter_near(chunk, rail):
+        lanes = rail_cols(rail)
+        scatter[chunk][rail][1].wait_recv()
+        for i in (0, 1):
+            a, b = (y, i) if rail == 0 else (i, x)
+            sums[chunk, a, b, :, lanes] = (
+                f32(sums[chunk, a, b, :, lanes]) + f32(first[chunk, rail, i])
+            ).astype(jnp.bfloat16)
+        begin(scatter[chunk][rail][2])
+
+    def scatter_end(chunk, rail):
+        lanes = rail_cols(rail)
+        scatter[chunk][rail][2].wait_recv()
+        feed = f32(sums[chunk, y, x, :, lanes]) + f32(second[chunk, rail])
+        mixed = f32(normed[chunk, row_slice(r, rows), lanes]) / f32(gain_ref[:, lanes])
+        token = lax.broadcasted_iota(jnp.int32, (rows, half), 0) + chunk * rows
+        out_ref[pl.ds(chunk * rows, rows), lanes] = jnp.where(
+            token < suffix_len[0], mixed + feed, 0.0
+        ).astype(jnp.bfloat16)
+
+    tiles = gate_w.shape[1] // tile
+    project(0)
+    project(1)
+    token_gather[0].forward()
+    token_gather[0].relay()
+    token_gather[0].finish()
+    norms(0)
+    for copy in weights:
+        copy.wait()
+    widen(0, 0, tiles // 2)
+    token_gather[1].forward()
+    widen(0, tiles // 2, tiles)
+    token_gather[1].relay()
+    narrow(0, 0)
+    scatter_core(0, 0)
+    narrow(0, 1)
+    scatter_core(0, 1)
+    scatter_far(0, 0)
+    token_gather[1].finish()
+    norms(1)
+    scatter_far(0, 1)
+    widen(1, 0, tiles // 2)
+    widen(1, tiles // 2, tiles)
+    scatter_near(0, 0)
+    scatter_near(0, 1)
+    narrow(1, 0)
+    scatter_core(1, 0)
+    narrow(1, 1)
+    scatter_core(1, 1)
+    scatter_far(1, 0)
+    scatter_far(1, 1)
+    scatter_end(0, 0)
+    scatter_end(0, 1)
+    scatter_near(1, 0)
+    scatter_near(1, 1)
+    scatter_end(1, 0)
+    scatter_end(1, 1)
+
+    for copy in started:
+        copy.wait_send()
+    for step in range(1, n_group):
+        for direction in (0, 1):
+
+            @pl.when(z_sends(direction, step))
+            def _():
+                z_copy(direction, step).wait_send()
+
+
+def fused(n_group, *args):
+    (
+        layer_input,
+        queries,
+        suffix_kv,
+        past_kv,
+        prefix_kv,
+        suffix_len,
+        past_len,
+        out_weight,
+        norm_gain,
+        gate_weight,
+        up_weight,
+        down_weight,
+    ) = args
+    n_req = 8
+    tokens, width = queries.shape
+    rows = tokens // CHUNKS
+    cols = width // n_req
+    ff = gate_weight.shape[1]
+    keys = n_req * prefix_kv.shape[0] + past_kv.shape[0] + tokens
+    half = width // 2
+    bf16, f32 = jnp.bfloat16, jnp.float32
+    hbm = pl.BlockSpec(memory_space=pl.ANY)
+    smem = pl.BlockSpec(memory_space=pltpu.SMEM)
+    vmem = pl.BlockSpec(memory_space=pltpu.VMEM)
+    n_copies = 2 * (n_req - 1) + 14 * 2 * CHUNKS + 6 * CHUNKS
+    return pl.pallas_call(
+        functools.partial(layer_kernel, n_group),
+        out_shape=jax.ShapeDtypeStruct((tokens, width), bf16),
+        in_specs=[hbm, hbm, hbm, hbm, hbm, smem, smem, hbm, vmem, hbm, hbm, hbm],
+        out_specs=vmem,
+        scratch_shapes=[
+            pltpu.VMEM((tokens, width), bf16),
+            pltpu.VMEM((keys, suffix_kv.shape[1]), bf16),
+            pltpu.VMEM((CHUNKS, HEADS // KV_HEADS * rows, keys), f32),
+            pltpu.VMEM((n_req, tokens, cols), bf16),
+            pltpu.VMEM((n_group * out_weight.shape[0], cols), bf16),
+            pltpu.VMEM((CHUNKS, n_req * rows, width), bf16),
+            pltpu.VMEM((CHUNKS, n_req * rows, width), bf16),
+            pltpu.VMEM((width, ff), bf16),
+            pltpu.VMEM((width, ff), bf16),
+            pltpu.VMEM((ff, width), bf16),
+            pltpu.VMEM((n_req * rows, ff), bf16),
+            pltpu.VMEM((n_req * rows, 1), f32),
+            pltpu.VMEM((CHUNKS, 2, 2, 2, rows, width), bf16),
+            pltpu.VMEM((CHUNKS, 2, 2, rows, width), bf16),
+            pltpu.VMEM((CHUNKS, 2, 2, rows, half), bf16),
+            pltpu.VMEM((CHUNKS, 2, rows, half), bf16),
+            pltpu.SemaphoreType.DMA((9,)),
+            pltpu.SemaphoreType.DMA((n_copies,)),
+            pltpu.SemaphoreType.DMA((n_copies,)),
+            pltpu.SemaphoreType.DMA((2, n_group - 1)),
+            pltpu.SemaphoreType.DMA((2, n_group - 1)),
+        ],
+        compiler_params=pltpu.CompilerParams(
+            collective_id=0, has_side_effects=True, vmem_limit_bytes=62 * 2**20
+        ),
+    )(
+        layer_input,
+        queries,
+        suffix_kv,
+        past_kv,
+        prefix_kv,
+        suffix_len,
+        past_len,
+        out_weight,
+        norm_gain.reshape(1, width),
+        gate_weight,
+        up_weight,
+        down_weight,
+    )
+
+
 def solution(mesh):
     in_specs = (
         P(("group", "req"), None),
@@ -125,4 +661,5 @@
         P("req", None),
     )
     out_specs = P(("group", "req"), None)
-    return jax.shard_map(shards, mesh=mesh, in_specs=in_specs, out_specs=out_specs, check_vma=False)
+    body = functools.partial(fused, mesh.shape["group"]) if dict(mesh.shape) == {"group": 4, "req": 8} else shards
+    return jax.shard_map(body, mesh=mesh, in_specs=in_specs, out_specs=out_specs, check_vma=False)

time: 271 us -> 141 us (0.52)
  waiting for transfers between devices: 165 us -> 0 us
  Pallas kernels: 0 us -> 136 us
  matrix products: 41.4 us -> 0 us
  blocking collectives: 36.6 us -> 0 us
  between operations: 14.8 us -> 1.31 us
  other arithmetic: 8.23 us -> 0 us
    pallas_call x0 -> x1, Pallas kernels: none -> 136 us  [fused(): pl.pallas_call(functools.partial(layer_kernel, n_group), out_shape=jax.Sh...]
    reduce_scatter x2 -> x0, waiting for transfers between devices: 119 us -> none  [the longest x1 61.2 us: shards(): lax.psum_scatter(jnp.dot(hidden, down_weight, preferred_element_type=jnp....]
    all_gather x1 -> x0, waiting for transfers between devices: 45.5 us -> none  [shards(): gathered = lax.all_gather(normed, 'req', axis=0, tiled=True)]
    dot_general x8 -> x0, matrix products: 41.4 us -> none  [the longest x1 11.3 us: shards(): gate = jnp.dot(picked, gate_weight, preferred_element_type=jnp.float32)]
    all_to_all x1 -> x0, blocking collectives: 25.3 us -> none  [shards(): lax.all_to_all(split_rows, 'group', split_axis=1, concat_axis=0, tiled=True)]
    all_gather x1 -> x0, blocking collectives: 11.3 us -> none  [shards(): piece = lax.all_gather(prefix_kv, 'req', axis=0, tiled=True)]
    convert_element_type x3 -> x0, other arithmetic: 4.73 us -> none  [the longest x1 2.39 us: shards(): return jnp.where(live[:, None], mixed + feed, 0.0).astype(jnp.bfloat16)]
    reduce_sum x3 -> x0, other arithmetic: 2.94 us -> none  [the longest x2 1.47 us: absorb(): totals = totals * factor + jnp.sum(expo, axis=-1)]
  transfers between devices with their start and end apart: 3 -> 0, of which waited for: 3 -> 0; matrix products, arithmetic and copies ran while one was open for 0% -> 0% of each run, Pallas kernels for 0% -> 0%
where the time goes in v1:
time: 141 us; the launch traced here: 140 us
  Pallas kernels  136 us (96%)
  local copies, waits for them, and re-layouts  3.36 us (2%)
    pallas_call x1, Pallas kernels, fused(): pl.pallas_call(functools.partial(layer_kernel, n_group), out_shape=jax.Sh...  136 us

profile of v1, /device:TPU:0, one launch (start us, length us, event | category | flops | bytes accessed | tf_op | source)
XLA Modules:
  0.0 140.4 jit_solution(653276469955797973)
XLA Ops:
  1.3 1.3 reshape.3.gain_ref
  2.6 135.7 %shard_map.118 = bf16[128,3072]{1,0:T(8,128)(2,1)} custom-call(bf16[128,3072]{1,0:T(8,128)(2,1)} %input_hbm.1, bf16[128,3072]{1,0:T(8,128)(2,1)} %query_hbm.1, bf16[128,2048]{1,0:T(8,128)(2,1)} %suffix_hbm.1, bf16[256,2048]{1,0:T(8,128)(2,1)} %past_hbm.1, bf16[16,2048]{1,0:T(8,128)(2,1)} %prefix_hbm.1, s32[1]{0:T(128)S(6)} %copy.14.suffix_len, ...), custom_call_target="tpu_custom_call" | custom-call | tf_op jit(solution)/shard_map/pallas_call | solution.py:601
  138.3 2.1 %copy.16 = bf16[128,3072]{1,0:T(8,128)(2,1)} copy(bf16[128,3072]{1,0:T(8,128)(2,1)} %shard_map.118) | data formatting | bytes 1572864

commit v2 on v1

--- a/solution.py
+++ b/solution.py
@@ -13,6 +13,8 @@
 SINK = 4
 MESH = pl.DeviceIdType.MESH
 CHUNKS = 2
+Z_PARTS = 2
+PIECES = 4
 
 
 def absorb(state, query_heads, key_rows, key_pos, key_valid, query_pos, window):
@@ -151,6 +153,7 @@
     recv_sem,
     z_send,
     z_recv,
+    gain,
 ):
     n_req = 8
     z = lax.axis_index("group")
@@ -240,15 +243,18 @@
         begin(copy)
         prefix_copies.append(copy)
 
-    def z_copy(direction, step):
+    def z_part(block, part):
+        return pl.ds(pl.multiple_of(block * depth + part * (depth // Z_PARTS), 16), depth // Z_PARTS)
+
+    def z_copy(direction, step, part):
         block = z - (step - 1) if direction == 0 else z + (step - 1)
-        where = out_w.at[row_slice(block, depth)]
-        src = outw_hbm.at[:, col_slice(r)] if step == 1 else where
+        where = out_w.at[z_part(block, part)]
+        src = outw_hbm.at[z_part(0, part), col_slice(r)] if step == 1 else where
         return pltpu.make_async_remote_copy(
             src_ref=src,
             dst_ref=where,
-            send_sem=z_send.at[direction, step - 1],
-            recv_sem=z_recv.at[direction, step - 1],
+            send_sem=z_send.at[direction, step - 1, part],
+            recv_sem=z_recv.at[direction, step - 1, part],
             device_id={"group": z + 1 if direction == 0 else z - 1},
             device_id_type=MESH,
         )
@@ -261,33 +267,34 @@
     def z_gets(direction, step):
         return z - step >= 0 if direction == 0 else z + step <= n_group - 1
 
-    def z_arrived(direction, step):
+    def z_arrived(direction, step, part):
         block = z - step if direction == 0 else z + step
-        where = out_w.at[row_slice(block, depth)]
+        where = out_w.at[z_part(block, part)]
         pltpu.make_async_remote_copy(
             src_ref=where,
             dst_ref=where,
-            send_sem=z_send.at[direction, step - 1],
-            recv_sem=z_recv.at[direction, step - 1],
+            send_sem=z_send.at[direction, step - 1, part],
+            recv_sem=z_recv.at[direction, step - 1, part],
             device_id={"req": flip(1)},
             device_id_type=MESH,
         ).wait_recv()
 
-    def z_step(step):
+    def z_step(step, part):
         for direction in (0, 1):
             if step > 1:
 
                 @pl.when(z_gets(direction, step - 1))
                 def _():
-                    z_arrived(direction, step - 1)
+                    z_arrived(direction, step - 1, part)
 
             if step < n_group:
 
                 @pl.when(z_sends(direction, step))
                 def _():
-                    z_copy(direction, step).start()
-
-    z_step(1)
+                    z_copy(direction, step, part).start()
+
+    z_step(1, 0)
+    z_step(1, 1)
 
     input_copies = []
     base = reserve(n_req - 1)
@@ -302,6 +309,8 @@
         local(up_hbm, up_w, 7),
         local(down_hbm, down_w, 8),
     ]
+
+    gain[...] = gain_ref[...].astype(jnp.float32).reshape(gain.shape)
 
     ratio = HEADS // KV_HEADS
     past_count = past_len[0]
@@ -338,8 +347,8 @@
         scores = scores * HEAD ** (-0.5) + bias[chunk]
         expo = jnp.exp(scores - jnp.max(scores, axis=-1, keepdims=True))
         denom = jnp.sum(expo, axis=-1, keepdims=True)
-        result = jnp.dot(expo.astype(jnp.bfloat16), values, preferred_element_type=jnp.float32) / denom
-        result = result.astype(jnp.bfloat16)
+        result = jnp.dot(expo.astype(jnp.bfloat16), values, preferred_element_type=jnp.float32)
+        result = (result * (1.0 / denom)).astype(jnp.bfloat16)
         for head in range(ratio):
             attended[chunk, row_slice(r, rows), pl.ds(lanes + head * HEAD, HEAD)] = result[
                 head * rows : (head + 1) * rows
@@ -401,23 +410,24 @@
 
     for chunk in range(CHUNKS):
 
-        @pl.loop(0, KV_HEADS // 2)
+        @pl.loop(0, KV_HEADS // 2, unroll=4)
         def _(group):
             attend(chunk, group)
 
         heads_gather[chunk].go(0, 3, 6)
 
-        @pl.loop(KV_HEADS // 2, KV_HEADS)
+        @pl.loop(KV_HEADS // 2, KV_HEADS, unroll=4)
         def _(group):
             attend(chunk, group)
 
         heads_gather[chunk].go(1, 2, 7)
-
-    z_step(2)
+        z_step(2, chunk)
+
     heads_gather[0].forward()
+    z_step(3, 0)
     heads_gather[0].relay()
-    z_step(3)
     heads_gather[1].forward()
+    z_step(3, 1)
     heads_gather[1].relay()
     for copy in input_copies:
         copy.wait_recv()
@@ -425,9 +435,10 @@
     own_w.wait()
     heads_gather[0].finish()
     heads_gather[1].finish()
-    z_step(4)
-
-    gain_here = gain_ref[:, col_slice(r)].astype(jnp.float32)
+    z_step(4, 0)
+    z_step(4, 1)
+
+    gain_here = gain[:, col_slice(r)]
 
     def project(chunk):
         total = jnp.dot(attended[chunk], out_w[...], preferred_element_type=jnp.float32)
@@ -438,7 +449,7 @@
         token_gather[chunk].go(0, 1, 2, 3, 6, 7)
 
     def norms(chunk):
-        inverse = 1.0 / gain_ref[...].astype(jnp.float32)
+        inverse = 1.0 / gain[...]
 
         @pl.loop(0, n_req)
         def _(block):
@@ -459,17 +470,17 @@
             gate = gate * scale
             hidden[:, lanes] = (gate / (1.0 + jnp.exp(-gate)) * (upper * scale)).astype(jnp.bfloat16)
 
-    def narrow(chunk, rail):
-        step = 512
-
-        @pl.loop(0, half // step)
+    span = width // PIECES
+
+    def narrow(chunk, piece):
+        @pl.loop(0, span // tile)
         def _(i):
-            lanes = pl.ds(pl.multiple_of(rail * half + i * step, 128), step)
+            lanes = pl.ds(pl.multiple_of(piece * span + i * tile, 128), tile)
             part = jnp.dot(hidden[...], down_w[:, lanes], preferred_element_type=jnp.float32)
-            parts[chunk, :, :, :, :, lanes] = part.astype(jnp.bfloat16).reshape(2, 2, 2, rows, step)
-
-    def rail_cols(rail):
-        return pl.ds(rail * half, half)
+            parts[chunk, :, :, :, :, lanes] = part.astype(jnp.bfloat16).reshape(2, 2, 2, rows, tile)
+
+    def rail_cols(piece):
+        return pl.ds(piece * span, span)
 
     def scatter_copies(chunk, rail):
         lanes = rail_cols(rail)
@@ -477,7 +488,7 @@
         to_core = remote(
             parts.at[chunk, :, :, 1 - core, :, lanes], sums.at[chunk, :, :, :, lanes], base, flip(1)
         )
-        if rail == 0:
+        if rail % 2 == 0:
             far = remote(sums.at[chunk, 1 - y, :, :, lanes], first.at[chunk, rail], base + 1, flip(4))
             near = remote(sums.at[chunk, y, 1 - x, :, lanes], second.at[chunk, rail], base + 2, flip(2))
         else:
@@ -485,7 +496,7 @@
             near = remote(sums.at[chunk, 1 - y, x, :, lanes], second.at[chunk, rail], base + 2, flip(4))
         return to_core, far, near
 
-    scatter = [[scatter_copies(chunk, rail) for rail in (0, 1)] for chunk in range(CHUNKS)]
+    scatter = [[scatter_copies(chunk, rail) for rail in range(PIECES)] for chunk in range(CHUNKS)]
 
     def f32(value):
         return value.astype(jnp.float32)
@@ -507,7 +518,7 @@
         lanes = rail_cols(rail)
         scatter[chunk][rail][1].wait_recv()
         for i in (0, 1):
-            a, b = (y, i) if rail == 0 else (i, x)
+            a, b = (y, i) if rail % 2 == 0 else (i, x)
             sums[chunk, a, b, :, lanes] = (
                 f32(sums[chunk, a, b, :, lanes]) + f32(first[chunk, rail, i])
             ).astype(jnp.bfloat16)
@@ -517,8 +528,8 @@
         lanes = rail_cols(rail)
         scatter[chunk][rail][2].wait_recv()
         feed = f32(sums[chunk, y, x, :, lanes]) + f32(second[chunk, rail])
-        mixed = f32(normed[chunk, row_slice(r, rows), lanes]) / f32(gain_ref[:, lanes])
-        token = lax.broadcasted_iota(jnp.int32, (rows, half), 0) + chunk * rows
+        mixed = f32(normed[chunk, row_slice(r, rows), lanes]) / gain[:, lanes]
+        token = lax.broadcasted_iota(jnp.int32, (rows, span), 0) + chunk * rows
         out_ref[pl.ds(chunk * rows, rows), lanes] = jnp.where(
             token < suffix_len[0], mixed + feed, 0.0
         ).astype(jnp.bfloat16)
@@ -536,39 +547,43 @@
     token_gather[1].forward()
     widen(0, tiles // 2, tiles)
     token_gather[1].relay()
-    narrow(0, 0)
-    scatter_core(0, 0)
-    narrow(0, 1)
-    scatter_core(0, 1)
-    scatter_far(0, 0)
+    for piece in range(PIECES):
+        narrow(0, piece)
+        scatter_core(0, piece)
+        if piece > 0:
+            scatter_far(0, piece - 1)
     token_gather[1].finish()
     norms(1)
-    scatter_far(0, 1)
+    scatter_far(0, PIECES - 1)
     widen(1, 0, tiles // 2)
-    widen(1, tiles // 2, tiles)
     scatter_near(0, 0)
     scatter_near(0, 1)
-    narrow(1, 0)
-    scatter_core(1, 0)
-    narrow(1, 1)
-    scatter_core(1, 1)
-    scatter_far(1, 0)
-    scatter_far(1, 1)
-    scatter_end(0, 0)
-    scatter_end(0, 1)
+    widen(1, tiles // 2, tiles)
+    scatter_near(0, 2)
+    scatter_near(0, 3)
+    for piece in range(PIECES):
+        narrow(1, piece)
+        scatter_core(1, piece)
+        if piece > 0:
+            scatter_far(1, piece - 1)
     scatter_near(1, 0)
-    scatter_near(1, 1)
-    scatter_end(1, 0)
-    scatter_end(1, 1)
+    scatter_far(1, PIECES - 1)
+    for piece in range(PIECES):
+        scatter_end(0, piece)
+    for piece in range(1, PIECES):
+        scatter_near(1, piece)
+        scatter_end(1, piece - 1)
+    scatter_end(1, PIECES - 1)
 
     for copy in started:
         copy.wait_send()
     for step in range(1, n_group):
-        for direction in (0, 1):
-
-            @pl.when(z_sends(direction, step))
-            def _():
-                z_copy(direction, step).wait_send()
+        for part in range(Z_PARTS):
+            for direction in (0, 1):
+
+                @pl.when(z_sends(direction, step))
+                def _():
+                    z_copy(direction, step, part).wait_send()
 
 
 def fused(n_group, *args):
@@ -592,12 +607,12 @@
     cols = width // n_req
     ff = gate_weight.shape[1]
     keys = n_req * prefix_kv.shape[0] + past_kv.shape[0] + tokens
-    half = width // 2
     bf16, f32 = jnp.bfloat16, jnp.float32
     hbm = pl.BlockSpec(memory_space=pl.ANY)
     smem = pl.BlockSpec(memory_space=pltpu.SMEM)
     vmem = pl.BlockSpec(memory_space=pltpu.VMEM)
-    n_copies = 2 * (n_req - 1) + 14 * 2 * CHUNKS + 6 * CHUNKS
+    n_copies = 2 * (n_req - 1) + 14 * 2 * CHUNKS + 3 * PIECES * CHUNKS
+    span = width // PIECES
     return pl.pallas_call(
         functools.partial(layer_kernel, n_group),
         out_shape=jax.ShapeDtypeStruct((tokens, width), bf16),
@@ -618,13 +633,14 @@
             pltpu.VMEM((n_req * rows, 1), f32),
             pltpu.VMEM((CHUNKS, 2, 2, 2, rows, width), bf16),
             pltpu.VMEM((CHUNKS, 2, 2, rows, width), bf16),
-            pltpu.VMEM((CHUNKS, 2, 2, rows, half), bf16),
-            pltpu.VMEM((CHUNKS, 2, rows, half), bf16),
+            pltpu.VMEM((CHUNKS, PIECES, 2, rows, span), bf16),
+            pltpu.VMEM((CHUNKS, PIECES, rows, span), bf16),
             pltpu.SemaphoreType.DMA((9,)),
             pltpu.SemaphoreType.DMA((n_copies,)),
             pltpu.SemaphoreType.DMA((n_copies,)),
-            pltpu.SemaphoreType.DMA((2, n_group - 1)),
-            pltpu.SemaphoreType.DMA((2, n_group - 1)),
+            pltpu.SemaphoreType.DMA((2, n_group - 1, Z_PARTS)),
+            pltpu.SemaphoreType.DMA((2, n_group - 1, Z_PARTS)),
+            pltpu.VMEM((1, width), f32),
         ],
         compiler_params=pltpu.CompilerParams(
             collective_id=0, has_side_effects=True, vmem_limit_bytes=62 * 2**20
@@ -638,7 +654,7 @@
         suffix_len,
         past_len,
         out_weight,
-        norm_gain.reshape(1, width),
+        norm_gain,
         gate_weight,
         up_weight,
         down_weight,

time: 141 us -> 131 us (0.929)
  Pallas kernels: 136 us -> 127 us
    pallas_call x1, Pallas kernels: 136 us -> 127 us  [fused(): pl.pallas_call(functools.partial(layer_kernel, n_group), out_shape=jax.Sh...]
where the time goes in v2:
time: 131 us; the launch traced here: 130 us
  Pallas kernels  127 us (97%)
  local copies, waits for them, and re-layouts  2.06 us (2%)
  between operations  1.31 us (1%)
    pallas_call x1, Pallas kernels, fused(): pl.pallas_call(functools.partial(layer_kernel, n_group), out_shape=jax.Sh...  127 us

profile of v2, /device:TPU:0, one launch (start us, length us, event | category | flops | bytes accessed | tf_op | source)
XLA Modules:
  0.0 130.3 jit_solution(14971281473263584384)
XLA Ops:
  1.3 126.9 %shard_map.118 = bf16[128,3072]{1,0:T(8,128)(2,1)} custom-call(bf16[128,3072]{1,0:T(8,128)(2,1)} %input_hbm.1, bf16[128,3072]{1,0:T(8,128)(2,1)} %query_hbm.1, bf16[128,2048]{1,0:T(8,128)(2,1)} %suffix_hbm.1, bf16[256,2048]{1,0:T(8,128)(2,1)} %past_hbm.1, bf16[16,2048]{1,0:T(8,128)(2,1)} %prefix_hbm.1, s32[1]{0:T(128)S(6)} %copy.14.suffix_len, ...), custom_call_target="tpu_custom_call" | custom-call | tf_op jit(solution)/shard_map/pallas_call | solution.py:616
  128.2 2.1 %copy.16 = bf16[128,3072]{1,0:T(8,128)(2,1)} copy(bf16[128,3072]{1,0:T(8,128)(2,1)} %shard_map.118) | data formatting | bytes 1572864

commit v3 on v2

--- a/solution.py
+++ b/solution.py
@@ -154,6 +154,8 @@
     z_send,
     z_recv,
     gain,
+    gate_sum,
+    up_sum,
 ):
     n_req = 8
     z = lax.axis_index("group")
@@ -296,14 +298,6 @@
     z_step(1, 0)
     z_step(1, 1)
 
-    input_copies = []
-    base = reserve(n_req - 1)
-    for mask in range(1, n_req):
-        other = flip(mask)
-        copy = remote(input_hbm.at[:, col_slice(other)], residual.at[r], base + mask - 1, other)
-        begin(copy)
-        input_copies.append(copy)
-
     weights = [
         local(gate_hbm, gate_w, 6),
         local(up_hbm, up_w, 7),
@@ -329,6 +323,14 @@
         copy.wait()
     for copy in prefix_copies:
         copy.wait_recv()
+
+    input_copies = []
+    base = reserve(n_req - 1)
+    for mask in range(1, n_req):
+        other = flip(mask)
+        copy = remote(input_hbm.at[:, col_slice(other)], residual.at[r], base + mask - 1, other)
+        begin(copy)
+        input_copies.append(copy)
 
     def attend(chunk, group):
         lanes = pl.multiple_of(group * (ratio * HEAD), 128)
@@ -446,7 +448,6 @@
             n_req * rows, cols
         )
         normed[chunk, :, col_slice(r)] = (total * gain_here).astype(jnp.bfloat16)
-        token_gather[chunk].go(0, 1, 2, 3, 6, 7)
 
     def norms(chunk):
         inverse = 1.0 / gain[...]
@@ -460,20 +461,41 @@
 
     tile = 256
 
+    def activate(gate, upper, lanes):
+        scale = row_scale[...]
+        gate = gate * scale
+        hidden[:, lanes] = (gate / (1.0 + jnp.exp(-gate)) * (upper * scale)).astype(jnp.bfloat16)
+
+    def widen_part(chunk, owner, is_first, is_last):
+        depth_here = pl.ds(pl.multiple_of(owner // 2 * (2 * cols), 128), 2 * cols)
+
+        @pl.loop(0, gate_w.shape[1] // tile, unroll=2)
+        def _(i):
+            lanes = pl.ds(pl.multiple_of(i * tile, 128), tile)
+            left = normed[chunk, :, depth_here]
+            gate = jnp.dot(left, gate_w[depth_here, lanes], preferred_element_type=jnp.float32)
+            upper = jnp.dot(left, up_w[depth_here, lanes], preferred_element_type=jnp.float32)
+            if not is_first:
+                gate = gate_sum[:, lanes] + gate
+                upper = up_sum[:, lanes] + upper
+            if is_last:
+                activate(gate, upper, lanes)
+            else:
+                gate_sum[:, lanes] = gate
+                up_sum[:, lanes] = upper
+
     def widen(chunk, start, stop):
-        @pl.loop(start, stop)
+        @pl.loop(start, stop, unroll=stop - start)
         def _(i):
             lanes = pl.ds(pl.multiple_of(i * tile, 128), tile)
             gate = jnp.dot(normed[chunk], gate_w[:, lanes], preferred_element_type=jnp.float32)
             upper = jnp.dot(normed[chunk], up_w[:, lanes], preferred_element_type=jnp.float32)
-            scale = row_scale[...]
-            gate = gate * scale
-            hidden[:, lanes] = (gate / (1.0 + jnp.exp(-gate)) * (upper * scale)).astype(jnp.bfloat16)
+            activate(gate, upper, lanes)
 
     span = width // PIECES
 
     def narrow(chunk, piece):
-        @pl.loop(0, span // tile)
+        @pl.loop(0, span // tile, unroll=span // tile)
         def _(i):
             lanes = pl.ds(pl.multiple_of(piece * span + i * tile, 128), tile)
             part = jnp.dot(hidden[...], down_w[:, lanes], preferred_element_type=jnp.float32)
@@ -535,19 +557,29 @@
         ).astype(jnp.bfloat16)
 
     tiles = gate_w.shape[1] // tile
+    order = (0, 1, 2, 3, 6, 7)
+    ahead = token_gather[0]
     project(0)
+    ahead.go(*order)
     project(1)
-    token_gather[0].forward()
-    token_gather[0].relay()
-    token_gather[0].finish()
-    norms(0)
     for copy in weights:
         copy.wait()
-    widen(0, 0, tiles // 2)
+    ahead.got(6, 7)
+    widen_part(0, r, True, False)
+    ahead.forward()
+    token_gather[1].go(*order)
+    ahead.got(8, 10)
+    widen_part(0, flip(2), False, False)
+    ahead.relay()
+    ahead.got(9, 11)
+    widen_part(0, flip(4), False, False)
+    ahead.got(12, 13)
+    norms(0)
+    widen_part(0, flip(6), False, True)
     token_gather[1].forward()
-    widen(0, tiles // 2, tiles)
-    token_gather[1].relay()
     for piece in range(PIECES):
+        if piece == 2:
+            token_gather[1].relay()
         narrow(0, piece)
         scatter_core(0, piece)
         if piece > 0:
@@ -641,6 +673,8 @@
             pltpu.SemaphoreType.DMA((2, n_group - 1, Z_PARTS)),
             pltpu.SemaphoreType.DMA((2, n_group - 1, Z_PARTS)),
             pltpu.VMEM((1, width), f32),
+            pltpu.VMEM((n_req * rows, ff), f32),
+            pltpu.VMEM((n_req * rows, ff), f32),
         ],
         compiler_params=pltpu.CompilerParams(
             collective_id=0, has_side_effects=True, vmem_limit_bytes=62 * 2**20

time: 131 us -> 122 us (0.931)
  Pallas kernels: 127 us -> 118 us
    pallas_call x1, Pallas kernels: 127 us -> 118 us  [fused(): pl.pallas_call(functools.partial(layer_kernel, n_group), out_shape=jax.Sh...]
where the time goes in v3:
time: 122 us
  Pallas kernels  118 us (97%)
  local copies, waits for them, and re-layouts  2.06 us (2%)
  between operations  1.31 us (1%)
    pallas_call x1, Pallas kernels, fused(): pl.pallas_call(functools.partial(layer_kernel, n_group), out_shape=jax.Sh...  118 us

profile of v3, /device:TPU:0, one launch (start us, length us, event | category | flops | bytes accessed | tf_op | source)
XLA Modules:
  0.0 121.7 jit_solution(8764813832090095346)
XLA Ops:
  1.3 118.3 %shard_map.118 = bf16[128,3072]{1,0:T(8,128)(2,1)} custom-call(bf16[128,3072]{1,0:T(8,128)(2,1)} %input_hbm.1, bf16[128,3072]{1,0:T(8,128)(2,1)} %query_hbm.1, bf16[128,2048]{1,0:T(8,128)(2,1)} %suffix_hbm.1, bf16[256,2048]{1,0:T(8,128)(2,1)} %past_hbm.1, bf16[16,2048]{1,0:T(8,128)(2,1)} %prefix_hbm.1, s32[1]{0:T(128)S(6)} %copy.14.suffix_len, ...), custom_call_target="tpu_custom_call" | custom-call | tf_op jit(solution)/shard_map/pallas_call | solution.py:648
  119.6 2.1 %copy.16 = bf16[128,3072]{1,0:T(8,128)(2,1)} copy(bf16[128,3072]{1,0:T(8,128)(2,1)} %shard_map.118) | data formatting | bytes 1572864

commit v4 on v3

--- a/solution.py
+++ b/solution.py
@@ -14,7 +14,7 @@
 MESH = pl.DeviceIdType.MESH
 CHUNKS = 2
 Z_PARTS = 2
-PIECES = 4
+PIECES = 6
 
 
 def absorb(state, query_heads, key_rows, key_pos, key_valid, query_pos, window):
@@ -437,16 +437,36 @@
     own_w.wait()
     heads_gather[0].finish()
     heads_gather[1].finish()
-    z_step(4, 0)
-    z_step(4, 1)
+
+    def project_part(chunk, block):
+        lanes = pl.ds(chunk * cols, cols)
+        depth_here = pl.ds(pl.multiple_of(block * depth, 128), depth)
+        gate_sum[:, lanes] += jnp.dot(
+            attended[chunk, :, depth_here], out_w[depth_here, :], preferred_element_type=jnp.float32
+        )
+
+    for chunk in range(CHUNKS):
+        gate_sum[:, pl.ds(chunk * cols, cols)] = (
+            residual[:, pl.ds(chunk * rows, rows), :].astype(jnp.float32).reshape(n_req * rows, cols)
+        )
+        project_part(chunk, z)
+
+    for step in range(1, n_group):
+        if step == n_group - 1:
+            z_step(4, 0)
+            z_step(4, 1)
+        for direction in (0, 1):
+
+            @pl.when(z_gets(direction, step))
+            def _():
+                for chunk in range(CHUNKS):
+                    project_part(chunk, z - step if direction == 0 else z + step)
+
 
     gain_here = gain[:, col_slice(r)]
 
     def project(chunk):
-        total = jnp.dot(attended[chunk], out_w[...], preferred_element_type=jnp.float32)
-        total = total + residual[:, pl.ds(chunk * rows, rows), :].astype(jnp.float32).reshape(
-            n_req * rows, cols
-        )
+        total = gate_sum[:, pl.ds(chunk * cols, cols)]
         normed[chunk, :, col_slice(r)] = (total * gain_here).astype(jnp.bfloat16)
 
     def norms(chunk):
@@ -573,10 +593,10 @@
     ahead.relay()
     ahead.got(9, 11)
     widen_part(0, flip(4), False, False)
+    token_gather[1].forward()
     ahead.got(12, 13)
     norms(0)
     widen_part(0, flip(6), False, True)
-    token_gather[1].forward()
     for piece in range(PIECES):
         if piece == 2:
             token_gather[1].relay()
@@ -588,23 +608,25 @@
     norms(1)
     scatter_far(0, PIECES - 1)
     widen(1, 0, tiles // 2)
-    scatter_near(0, 0)
-    scatter_near(0, 1)
+    for piece in range(PIECES // 2):
+        scatter_near(0, piece)
     widen(1, tiles // 2, tiles)
-    scatter_near(0, 2)
-    scatter_near(0, 3)
+    for piece in range(PIECES // 2, PIECES):
+        scatter_near(0, piece)
     for piece in range(PIECES):
         narrow(1, piece)
         scatter_core(1, piece)
         if piece > 0:
             scatter_far(1, piece - 1)
+    scatter_far(1, PIECES - 1)
     scatter_near(1, 0)
-    scatter_far(1, PIECES - 1)
+    scatter_near(1, 1)
     for piece in range(PIECES):
         scatter_end(0, piece)
-    for piece in range(1, PIECES):
+    for piece in range(2, PIECES):
         scatter_near(1, piece)
-        scatter_end(1, piece - 1)
+        scatter_end(1, piece - 2)
+    scatter_end(1, PIECES - 2)
     scatter_end(1, PIECES - 1)
 
     for copy in started:

time: 122 us -> 124 us (1.016)
  Pallas kernels: 118 us -> 121 us
    pallas_call x1, Pallas kernels: 118 us -> 121 us  [fused(): pl.pallas_call(functools.partial(layer_kernel, n_group), out_shape=jax.Sh...]
where the time goes in v4:
time: 124 us
  Pallas kernels  121 us (98%)
  local copies, waits for them, and re-layouts  2.06 us (2%)
  between operations  1.31 us (1%)
    pallas_call x1, Pallas kernels, fused(): pl.pallas_call(functools.partial(layer_kernel, n_group), out_shape=jax.Sh...  121 us

profile of v4, /device:TPU:0, one launch (start us, length us, event | category | flops | bytes accessed | tf_op | source)
XLA Modules:
  0.0 124.0 jit_solution(10117452936813057998)
XLA Ops:
  1.3 120.6 %shard_map.118 = bf16[128,3072]{1,0:T(8,128)(2,1)} custom-call(bf16[128,3072]{1,0:T(8,128)(2,1)} %input_hbm.1, bf16[128,3072]{1,0:T(8,128)(2,1)} %query_hbm.1, bf16[128,2048]{1,0:T(8,128)(2,1)} %suffix_hbm.1, bf16[256,2048]{1,0:T(8,128)(2,1)} %past_hbm.1, bf16[16,2048]{1,0:T(8,128)(2,1)} %prefix_hbm.1, s32[1]{0:T(128)S(6)} %copy.14.suffix_len, ...), custom_call_target="tpu_custom_call" | custom-call | tf_op jit(solution)/shard_map/pallas_call | solution.py:670
  121.9 2.1 %copy.16 = bf16[128,3072]{1,0:T(8,128)(2,1)} copy(bf16[128,3072]{1,0:T(8,128)(2,1)} %shard_map.118) | data formatting | bytes 1572864
